TPU v7x, 32 devices: a whole 2x2x4 slice. The times are simulated.
32 devices in a mesh: group: 4 (over z), sub: 8 (over y, x, core).
Axes of the slice: x: 2, y: 2, z: 4, core: 2. Of those that a mesh axis runs over, the one named last changes fastest.
Arguments:
- couplings: float32 [32, 6, 384, 384], P(('group', 'sub')), may hold values from -0.3125 to 0.3125
- mode_rows: float32 [49152, 128], P(('group', 'sub')), may hold values from -1.5 to 1.5
- coarse_basis: float32 [4096, 256], P(('group', 'sub')), may hold values from -0.1875 to 0.1875
- stiffness: float32 [32, 1536], P(('group', 'sub')), may hold values from 0.005 to 0.05
- own_face: int32 [32, 6], P(('group', 'sub')), may hold values from 0 to 3, as said below
- neighbour_face: int32 [32, 6], P(('group', 'sub')), may hold values from 0 to 3, as said below
- present: int32 [32, 6], P(('group', 'sub')), may hold values from 0 to 1, as said below
Outputs:
- coarse_blocks: float32 [32, 7, 128, 128], P(('group', 'sub'))
- coarse_group: float32 [4, 3, 256, 256], P('group', None, 'sub')
Inputs may be any that keep to these rules, and one draw needn't show every extreme that they name: `own_face`: face block index of the subdomain's own unknowns toward each direction. Wherever present is 1, neighbour_face[d, k] equals own_face of the neighbour n(d, k) at the opposite direction (0 and 1, 2 and 3, 4 and 5 are opposite). `present`: 0 wherever the neighbour lies outside the group's plane of 4 columns and 2 rows or outside the groups, and on broken couplings; a coupling is intact on both sides or on neither.
All inputs are finite; a program needn't handle non-finite values.
Results may differ from a plain program's by a relative error of at most 0.0003.
Values sent between devices are 32-bit elements; how exact they have to be, the bound alone decides.
A program may use at most 64 MiB of HBM per device.

v0:
```python
import jax
import jax.numpy as jnp
from jax import lax
from jax.sharding import PartitionSpec as P

DIRS = 6
SUB_ROW = 4


PRECISE = lax.Precision.HIGHEST


def from_behind(shard, axis, by):
    devices = lax.axis_size(axis)
    pairs = [(i, i + by) for i in range(devices) if 0 <= i + by < devices]
    return lax.ppermute(shard, axis, pairs)


def matmul(left, right):
    return jnp.dot(left, right, precision=PRECISE, preferred_element_type=jnp.float32)


def transposed_product(left, right):
    return lax.dot_general(
        left, right, (((0,), (0,)), ((), ())), precision=PRECISE, preferred_element_type=jnp.float32
    )


def fetch_plane(local_modes, local_basis, neighbour_face, direction, offset, block_size):
    got_modes, got_basis = from_behind((local_modes, local_basis), "sub", offset)
    far_part = lax.dynamic_slice_in_dim(
        got_modes, neighbour_face[0, direction] * block_size, block_size, 0
    )
    return (far_part, got_basis)


def fetch_stack(local_modes, local_basis, neighbour_face, direction, offset, block_size):
    got_modes, got_basis = from_behind((local_modes, local_basis), "group", offset)
    far_part = lax.dynamic_slice_in_dim(
        got_modes, neighbour_face[0, direction] * block_size, block_size, 0
    )
    return (far_part, got_basis)


def body(couplings, mode_rows, coarse_basis, stiffness, own_face, neighbour_face, present):
    block_size = couplings.shape[2]
    fetched = []
    for direction, offset in ((0, 1), (1, -1), (2, SUB_ROW), (3, -SUB_ROW)):
        fetched.append(
            fetch_plane(mode_rows, coarse_basis, neighbour_face, direction, offset, block_size)
        )
    for direction, offset in ((4, 1), (5, -1)):
        fetched.append(
            fetch_stack(mode_rows, coarse_basis, neighbour_face, direction, offset, block_size)
        )
    block_list = []
    projected = []
    for direction in range(DIRS):
        far_part, far_basis = fetched[direction]
        own_part = lax.dynamic_slice_in_dim(
            mode_rows, own_face[0, direction] * block_size, block_size, 0
        )
        weight = present[0, direction].astype(jnp.float32)
        product = matmul(couplings[0, direction], own_part)
        coarse_block = transposed_product(product, far_part) * weight
        block_list.append(coarse_block)
        projected.append(matmul(transposed_product(coarse_basis, coarse_block), far_basis))
    self_block = transposed_product(mode_rows * stiffness[0][:, None], mode_rows)
    block_list.append(self_block)
    within = matmul(transposed_product(coarse_basis, self_block), coarse_basis)
    within = within + projected[0] + projected[1] + projected[2] + projected[3]
    stacked = jnp.stack([projected[4], within, projected[5]])
    own_rows = lax.psum_scatter(stacked, "sub", scatter_dimension=1, tiled=True)
    return (jnp.stack(block_list)[None], own_rows[None])


def solution(mesh):
    return jax.shard_map(
        body,
        mesh=mesh,
        in_specs=(
            P(("group", "sub"), None, None, None),
            P(("group", "sub"), None),
            P(("group", "sub"), None),
            P(("group", "sub"), None),
            P(("group", "sub"), None),
            P(("group", "sub"), None),
            P(("group", "sub"), None),
        ),
        out_specs=(P(("group", "sub"), None, None, None), P("group", None, "sub", None)),
        check_vma=False,
    )
```

profile of v0, /device:TPU:0, one launch (start us, length us, event | category | flops | bytes accessed | tf_op | source)
XLA Modules:
  0.0 130.6 jit_solution(10405507148290349697)
XLA Ops:
  7.3 3.4 %collective-permute-start = (f32[1536,128]{1,0:T(8,128)}, f32[1536,128]{1,0:T(8,128)}, u32[]{:S(2)}, u32[]{:S(2)}) collective-permute-start(f32[1536,128]{1,0:T(8,128)} %param.8), channel_id=1, source_target_pairs={{0,1},{1,2},{2,3},{3,4},{4,5},{5,6},{6,7},{8,9},{9,10},{10,11},{11... | collective-permute-start | bytes 2359304 | tf_op jit(solution)/shard_map/ppermute | solution.py:16
  10.7 1.3 collective-permute-start.1
  11.9 7.7 %collective-permute-start.2 = (f32[1536,128]{1,0:T(8,128)}, f32[1536,128]{1,0:T(8,128)}, u32[]{:S(2)}, u32[]{:S(2)}) collective-permute-start(f32[1536,128]{1,0:T(8,128)} %param.8), channel_id=1, source_target_pairs={{0,4},{1,5},{2,6},{3,7},{8,12},{9,13},{10,14},{11,15},{16,20},{17,... | collective-permute-start | bytes 2359304 | tf_op jit(solution)/shard_map/ppermute | solution.py:16
  19.7 1.3 collective-permute-start.3
  21.0 3.5 %collective-permute-start.4 = (f32[1536,128]{1,0:T(8,128)}, f32[1536,128]{1,0:T(8,128)S(1)}, u32[]{:S(2)}, u32[]{:S(2)}) collective-permute-start(f32[1536,128]{1,0:T(8,128)} %param.8), channel_id=1, source_target_pairs={{0,8},{8,16},{16,24},{1,9},{9,17},{17,25},{2,10},{10,18},{18,26},{... | collective-permute-start | bytes 2359304 | tf_op jit(solution)/shard_map/ppermute | solution.py:16
  24.5 1.6 %fusion.50 = (s32[1,1]{1,0:T(1,128)}, s32[1,1]{1,0:T(1,128)}, s32[1,1]{1,0:T(1,128)}, s32[1,1]{1,0:T(1,128)}, s32[1,1]{1,0:T(1,128)}, /*index=5*/s32[1,1]{1,0:T(1,128)}) fusion(s32[1,6]{1,0:T(1,128)} %param.11), kind=kLoop, calls=%fused_computation.68 | loop fusion | bytes 48 | tf_op jit(solution)/shard_map/slice | solution.py:61
  26.6 1.6 %fusion.49 = (s32[1,1]{1,0:T(1,128)}, s32[1,1]{1,0:T(1,128)}, s32[1,1]{1,0:T(1,128)}, s32[1,1]{1,0:T(1,128)}, s32[1,1]{1,0:T(1,128)}, /*index=5*/s32[1,1]{1,0:T(1,128)}) fusion(s32[1,6]{1,0:T(1,128)} %param.12), kind=kLoop, calls=%fused_computation.67 | loop fusion | bytes 48 | tf_op jit(solution)/shard_map/slice | solution.py:40
  35.1 2.0 %fusion.15 = f32[128,384]{1,0:T(8,128)S(1)} fusion(f32[1,6,384,384]{3,2,1,0:T(8,128)} %param.7, f32[1536,128]{1,0:T(8,128)} %param.8, s32[]{:T(128)S(6)} %select_n.36), kind=kOutput, calls=%fused_computation.26 | convolution fusion | flops 226492416 | bytes 983044 | tf_op jit(solution)/shard_map/dot_general | solution.py:20
  37.1 2.0 %fusion.13 = f32[128,384]{1,0:T(8,128)S(1)} fusion(f32[1,6,384,384]{3,2,1,0:T(8,128)} %param.7, f32[1536,128]{1,0:T(8,128)} %param.8, s32[]{:T(128)S(6)} %select_n.38), kind=kOutput, calls=%fused_computation.24 | convolution fusion | flops 226492416 | bytes 983044 | tf_op jit(solution)/shard_map/dot_general | solution.py:20
  39.1 2.0 %fusion.11 = f32[128,384]{1,0:T(8,128)S(1)} fusion(f32[1,6,384,384]{3,2,1,0:T(8,128)} %param.7, f32[1536,128]{1,0:T(8,128)} %param.8, s32[]{:T(128)S(6)} %select_n.40), kind=kOutput, calls=%fused_computation.22 | convolution fusion | flops 226492416 | bytes 983044 | tf_op jit(solution)/shard_map/dot_general | solution.py:20
  41.1 2.0 %fusion.9 = f32[128,384]{1,0:T(8,128)S(1)} fusion(f32[1,6,384,384]{3,2,1,0:T(8,128)} %param.7, f32[1536,128]{1,0:T(8,128)} %param.8, s32[]{:T(128)S(6)} %select_n.42), kind=kOutput, calls=%fused_computation.20 | convolution fusion | flops 226492416 | bytes 983044 | tf_op jit(solution)/shard_map/dot_general | solution.py:20
  43.1 1.9 %fusion.7 = f32[128,384]{1,0:T(8,128)S(1)} fusion(f32[1,6,384,384]{3,2,1,0:T(8,128)} %param.7, f32[1536,128]{1,0:T(8,128)S(1)} %copy-done, s32[]{:T(128)S(6)} %select_n.44), kind=kOutput, calls=%fused_computation.18 | convolution fusion | flops 226492416 | bytes 983044 | tf_op jit(solution)/shard_map/dot_general | solution.py:20
  44.9 1.9 %fusion.5 = f32[128,384]{1,0:T(8,128)S(1)} fusion(f32[1,6,384,384]{3,2,1,0:T(8,128)} %param.7, f32[1536,128]{1,0:T(8,128)S(1)} %copy-done, s32[]{:T(128)S(6)} %select_n.46), kind=kOutput, calls=%fused_computation.16 | convolution fusion | flops 226492416 | bytes 983044 | tf_op jit(solution)/shard_map/dot_general | solution.py:20
  51.4 1.3 collective-permute-start.5
  52.7 1.2 bitcast_dynamic-update-slice_fusion.6
  54.0 1.3 collective-permute-start.7
  56.5 1.3 collective-permute-start.10
  59.1 6.0 %collective-permute-start.9 = (f32[128,256]{1,0:T(8,128)S(1)}, f32[128,256]{1,0:T(8,128)S(1)}, u32[]{:S(2)}, u32[]{:S(2)}) collective-permute-start(f32[128,256]{1,0:T(8,128)S(1)} %copy-done.1), channel_id=1, source_target_pairs={{0,4},{1,5},{2,6},{3,7},{8,12},{9,13},{10,14},{11,15},{16,20},{17,... | collective-permute-start | bytes 393224 | tf_op jit(solution)/shard_map/ppermute | solution.py:16
  66.4 1.3 collective-permute-start.8
  68.1 3.1 %collective-permute-done.5 = f32[1536,128]{1,0:T(8,128)S(1)} collective-permute-done((f32[1536,128]{1,0:T(8,128)S(1)}, f32[1536,128]{1,0:T(8,128)S(1)}, u32[]{:S(2)}, u32[]{:S(2)}) %collective-permute-start.5) | collective-permute-done | bytes 786464 | tf_op jit(solution)/shard_map/ppermute | solution.py:16
  71.1 1.3 collective-permute-start.11
  72.8 1.7 %bitcast_dynamic-update-slice_fusion = (f32[7,128,128]{2,1,0:T(8,128)S(1)}, f32[128,128]{1,0:T(8,128)S(1)}) fusion(f32[7,128,128]{2,1,0:T(8,128)S(1)} %get-tuple-element.30, f32[1536,128]{1,0:T(8,128)S(1)} %copy-done, f32[1536]{0:T(1024)S(1)} %reduce), kind=kOutput, calls=%fused_computation.47 | convolution fusion | flops 302186496 | bytes 1712128 | tf_op jit(solution)/shard_map/dot_general | solution.py:24
  76.2 4.7 %collective-permute-start.6 = (f32[128,256]{1,0:T(8,128)S(1)}, f32[128,256]{1,0:T(8,128)S(1)}, u32[]{:S(2)}, u32[]{:S(2)}) collective-permute-start(f32[128,256]{1,0:T(8,128)S(1)} %copy-done.1), channel_id=1, source_target_pairs={{0,8},{8,16},{16,24},{1,9},{9,17},{17,25},{2,10},{10,18},{18,26},{... | collective-permute-start | bytes 393224 | tf_op jit(solution)/shard_map/ppermute | solution.py:16
  85.4 38.4 %reduce-scatter.2.cloned.1.call-done = f32[3,32,256]{2,1,0:T(8,128)} async-done(((f32[3,256,256]{2,1,0:T(8,128)}), f32[3,32,256]{2,1,0:T(8,128)}) %reduce-scatter.2.cloned.1.call-update) | async-done | bytes 98320 | tf_op jit(solution)/shard_map/reduce_scatter | solution.py:73
  (45 shorter events, 11.2 us)
Async XLA Ops:
  7.2 35.9 %copy-start = (f32[1536,128]{1,0:T(8,128)S(1)}, f32[1536,128]{1,0:T(8,128)}, u32[]{:S(2)}) copy-start(f32[1536,128]{1,0:T(8,128)} %param.8) | copy-start | bytes 2359300
  7.2 39.6 %copy-start.2 = (s32[1,6]{1,0:T(1,128)S(1)}, s32[1,6]{1,0:T(1,128)}, u32[]{:S(2)}) copy-start(s32[1,6]{1,0:T(1,128)} %param.13) | copy-start | bytes 76
  7.2 44.2 %copy-start.4 = (f32[1,1536]{1,0:T(1,128)S(1)}, f32[1,1536]{1,0:T(1,128)}, u32[]{:S(2)}) copy-start(f32[1,1536]{1,0:T(1,128)} %param.10) | copy-start | bytes 18436
  7.2 46.8 %copy-start.1 = (f32[128,256]{1,0:T(8,128)S(1)}, f32[128,256]{1,0:T(8,128)}, u32[]{:S(2)}) copy-start(f32[128,256]{1,0:T(8,128)} %param.9) | copy-start | bytes 393220
  7.2 116.6 %reduce-scatter.2.cloned.1.call-start = ((), (), s32[]{:S(2)}) async-start(), calls=%async_computation.1 | async-start | bytes 884736 | tf_op jit(solution)/shard_map/reduce_scatter | solution.py:73
  7.3 44.1 %collective-permute-start = (f32[1536,128]{1,0:T(8,128)}, f32[1536,128]{1,0:T(8,128)}, u32[]{:S(2)}, u32[]{:S(2)}) collective-permute-start(f32[1536,128]{1,0:T(8,128)} %param.8), channel_id=1, source_target_pairs={{0,1},{1,2},{2,3},{3,4},{4,5},{5,6},{6,7},{8,9},{9,10},{10,11},{11... | collective-permute-start | bytes 2359304 | tf_op jit(solution)/shard_map/ppermute | solution.py:16
  10.7 43.3 %collective-permute-start.1 = (f32[1536,128]{1,0:T(8,128)}, f32[1536,128]{1,0:T(8,128)}, u32[]{:S(2)}, u32[]{:S(2)}) collective-permute-start(f32[1536,128]{1,0:T(8,128)} %param.8), channel_id=1, source_target_pairs={{1,0},{2,1},{3,2},{4,3},{5,4},{6,5},{7,6},{9,8},{10,9},{11,10},{12... | collective-permute-start | bytes 2359304 | tf_op jit(solution)/shard_map/ppermute | solution.py:16
  11.9 44.6 %collective-permute-start.2 = (f32[1536,128]{1,0:T(8,128)}, f32[1536,128]{1,0:T(8,128)}, u32[]{:S(2)}, u32[]{:S(2)}) collective-permute-start(f32[1536,128]{1,0:T(8,128)} %param.8), channel_id=1, source_target_pairs={{0,4},{1,5},{2,6},{3,7},{8,12},{9,13},{10,14},{11,15},{16,20},{17,... | collective-permute-start | bytes 2359304 | tf_op jit(solution)/shard_map/ppermute | solution.py:16
  19.7 39.4 %collective-permute-start.3 = (f32[1536,128]{1,0:T(8,128)}, f32[1536,128]{1,0:T(8,128)}, u32[]{:S(2)}, u32[]{:S(2)}) collective-permute-start(f32[1536,128]{1,0:T(8,128)} %param.8), channel_id=1, source_target_pairs={{4,0},{5,1},{6,2},{7,3},{12,8},{13,9},{14,10},{15,11},{20,16},{21,... | collective-permute-start | bytes 2359304 | tf_op jit(solution)/shard_map/ppermute | solution.py:16
  21.0 45.5 %collective-permute-start.4 = (f32[1536,128]{1,0:T(8,128)}, f32[1536,128]{1,0:T(8,128)S(1)}, u32[]{:S(2)}, u32[]{:S(2)}) collective-permute-start(f32[1536,128]{1,0:T(8,128)} %param.8), channel_id=1, source_target_pairs={{0,8},{8,16},{16,24},{1,9},{9,17},{17,25},{2,10},{10,18},{18,26},{... | collective-permute-start | bytes 2359304 | tf_op jit(solution)/shard_map/ppermute | solution.py:16
  51.4 19.8 %collective-permute-start.5 = (f32[1536,128]{1,0:T(8,128)S(1)}, f32[1536,128]{1,0:T(8,128)S(1)}, u32[]{:S(2)}, u32[]{:S(2)}) collective-permute-start(f32[1536,128]{1,0:T(8,128)S(1)} %copy-done), channel_id=1, source_target_pairs={{8,0},{16,8},{24,16},{9,1},{17,9},{25,17},{10,2},{18,10},{26,18},{... | collective-permute-start | bytes 2359304 | tf_op jit(solution)/shard_map/ppermute | solution.py:16
  54.0 28.4 %collective-permute-start.7 = (f32[128,256]{1,0:T(8,128)S(1)}, f32[128,256]{1,0:T(8,128)S(1)}, u32[]{:S(2)}, u32[]{:S(2)}) collective-permute-start(f32[128,256]{1,0:T(8,128)S(1)} %copy-done.1), channel_id=1, source_target_pairs={{0,1},{1,2},{2,3},{3,4},{4,5},{5,6},{6,7},{8,9},{9,10},{10,11},{11... | collective-permute-start | bytes 393224 | tf_op jit(solution)/shard_map/ppermute | solution.py:16
  56.5 19.6 %collective-permute-start.10 = (f32[128,256]{1,0:T(8,128)S(1)}, f32[128,256]{1,0:T(8,128)S(1)}, u32[]{:S(2)}, u32[]{:S(2)}) collective-permute-start(f32[128,256]{1,0:T(8,128)S(1)} %copy-done.1), channel_id=1, source_target_pairs={{4,0},{5,1},{6,2},{7,3},{12,8},{13,9},{14,10},{15,11},{20,16},{21,... | collective-permute-start | bytes 393224 | tf_op jit(solution)/shard_map/ppermute | solution.py:16
  59.1 22.5 %collective-permute-start.9 = (f32[128,256]{1,0:T(8,128)S(1)}, f32[128,256]{1,0:T(8,128)S(1)}, u32[]{:S(2)}, u32[]{:S(2)}) collective-permute-start(f32[128,256]{1,0:T(8,128)S(1)} %copy-done.1), channel_id=1, source_target_pairs={{0,4},{1,5},{2,6},{3,7},{8,12},{9,13},{10,14},{11,15},{16,20},{17,... | collective-permute-start | bytes 393224 | tf_op jit(solution)/shard_map/ppermute | solution.py:16
  66.4 17.6 %collective-permute-start.8 = (f32[128,256]{1,0:T(8,128)S(1)}, f32[128,256]{1,0:T(8,128)S(1)}, u32[]{:S(2)}, u32[]{:S(2)}) collective-permute-start(f32[128,256]{1,0:T(8,128)S(1)} %copy-done.1), channel_id=1, source_target_pairs={{1,0},{2,1},{3,2},{4,3},{5,4},{6,5},{7,6},{9,8},{10,9},{11,10},{12... | collective-permute-start | bytes 393224 | tf_op jit(solution)/shard_map/ppermute | solution.py:16
  71.1 12.0 %collective-permute-start.11 = (f32[128,256]{1,0:T(8,128)S(1)}, f32[128,256]{1,0:T(8,128)S(1)}, u32[]{:S(2)}, u32[]{:S(2)}) collective-permute-start(f32[128,256]{1,0:T(8,128)S(1)} %copy-done.1), channel_id=1, source_target_pairs={{8,0},{16,8},{24,16},{9,1},{17,9},{25,17},{10,2},{18,10},{26,18},{... | collective-permute-start | bytes 393224 | tf_op jit(solution)/shard_map/ppermute | solution.py:16
  74.5 10.9 %copy-start.3 = (f32[7,128,128]{2,1,0:T(8,128)}, f32[7,128,128]{2,1,0:T(8,128)S(1)}, u32[]{:S(2)}) copy-start(f32[7,128,128]{2,1,0:T(8,128)S(1)} %get-tuple-element.32) | copy-start | bytes 1376260
  76.2 7.4 %collective-permute-start.6 = (f32[128,256]{1,0:T(8,128)S(1)}, f32[128,256]{1,0:T(8,128)S(1)}, u32[]{:S(2)}, u32[]{:S(2)}) collective-permute-start(f32[128,256]{1,0:T(8,128)S(1)} %copy-done.1), channel_id=1, source_target_pairs={{0,8},{8,16},{16,24},{1,9},{9,17},{17,25},{2,10},{10,18},{18,26},{... | collective-permute-start | bytes 393224 | tf_op jit(solution)/shard_map/ppermute | solution.py:16
Sparse Core Ops, SparseCore 0:
  85.5 38.1 reduce-scatter.1
where the time goes:
time: 131 us
  waiting for transfers between devices  41.5 us (32%)
  starting transfers between devices  34.5 us (26%)
  between operations  25.8 us (20%)
  matrix products  24.1 us (18%)
  local copies, waits for them, and re-layouts  3.82 us (3%)
    reduce_scatter x1, waiting for transfers between devices, body(): own_rows = lax.psum_scatter(stacked, 'sub', scatter_dimension=1, tiled=True)  38.4 us
    ppermute x12, starting transfers between devices, from_behind(): return lax.ppermute(shard, axis, pairs)  34.4 us
    dot_general x13, matrix products, matmul(): jnp.dot(left, right, precision=PRECISE, preferred_element_type=jnp.float32)  14.6 us
    dot_general x14, matrix products, transposed_product(): lax.dot_general(left, right, (((0,), (0,)), ((), ())), precision=PRECISE,...  9.48 us
    ppermute x12, waiting for transfers between devices, from_behind(): return lax.ppermute(shard, axis, pairs)  3.12 us
  transfers between devices with their start and end apart: 13, of which 2 were waited for; matrix products, arithmetic and copies ran while one was open for 21% of the time, Pallas kernels for 0%

commit v1 on v0

v1 whole, which is shorter than its diff:
```python
import functools

import jax
import jax.numpy as jnp
from jax import lax
from jax.experimental import pallas as pl
from jax.experimental.pallas import tpu as pltpu
from jax.sharding import PartitionSpec as P

SUB_ROW = 4
F32 = jnp.float32
BF16 = jnp.bfloat16
MESH = pl.DeviceIdType.MESH


def split(value):
    high = value.astype(BF16)
    return high, (value - high.astype(F32)).astype(BF16)


def dot(left, right):
    return jnp.dot(left, right, preferred_element_type=F32)


def product(left, right):
    (lh, ll), (rh, rl) = left, right
    return dot(lh, rh) + (dot(lh, rl) + dot(ll, rh))


def bit_orders(bits):
    return (list(range(bits)), [0] + list(range(bits - 1, 0, -1)))


def block_order(order, subs):
    bits = len(order)
    return [
        sum(((p >> (bits - 1 - t)) & 1) << order[t] for t in range(bits)) for p in range(subs)
    ]


def kernel(
    groups, subs, dirs,
    own_face, present, couplings, mode_rows, coarse_basis, stiffness,
    blocks_out, group_out,
    tangent, modes, faces, far, basis, turned_hi, turned_lo, zt_hi, zt_lo, blocks, acc, got,
    load_sem, tangent_sem, out_sem, v_send, v_recv, z_send, z_recv, r_send, r_recv,
):
    block = tangent.shape[1]
    bits = subs.bit_length() - 1
    orders = bit_orders(bits)
    group, sub = lax.axis_index("group"), lax.axis_index("sub")
    column, row = sub % SUB_ROW, sub // SUB_ROW
    own = dirs

    loads = [
        pltpu.make_async_copy(mode_rows, modes, load_sem.at[0]),
        pltpu.make_async_copy(coarse_basis, basis.at[own], load_sem.at[1]),
    ]
    for load in loads:
        load.start()
    tangent_loads = [
        pltpu.make_async_copy(couplings.at[k], tangent.at[k], tangent_sem.at[k]) for k in range(dirs)
    ]
    for load in tangent_loads:
        load.start()

    has = [
        column > 0, column < SUB_ROW - 1,
        row > 0, row < subs // SUB_ROW - 1,
        group > 0, group < groups - 1,
    ]
    peers = [
        (group, sub - 1), (group, sub + 1),
        (group, sub - SUB_ROW), (group, sub + SUB_ROW),
        (group - 1, sub), (group + 1, sub),
    ]
    partners = []
    for bit in range(bits):
        mine = (sub // (1 << bit)) % 2
        partners.append((group, sub + (1 - 2 * mine) * (1 << bit)))

    barrier = pltpu.get_barrier_semaphore()
    expected = bits
    for k in range(dirs):
        expected = expected + has[k].astype(jnp.int32)

        @pl.when(has[k])
        def _(k=k):
            pl.semaphore_signal(barrier, inc=1, device_id=peers[k], device_id_type=MESH)

    for bit in range(bits):
        pl.semaphore_signal(barrier, inc=1, device_id=partners[bit], device_id_type=MESH)

    def v_copy(k, slot):
        return pltpu.make_async_remote_copy(
            src_ref=faces.at[k], dst_ref=far.at[slot], send_sem=v_send.at[k],
            recv_sem=v_recv.at[slot], device_id=peers[k], device_id_type=MESH,
        )

    def z_copy(k, slot):
        return pltpu.make_async_remote_copy(
            src_ref=basis.at[own], dst_ref=basis.at[slot], send_sem=z_send.at[k],
            recv_sem=z_recv.at[slot], device_id=peers[k], device_id_type=MESH,
        )

    sending = (4, 5, 2, 3, 0, 1)
    loads[0].wait()
    for k in sending:
        faces[k] = modes[own_face[0, k]]
    pl.semaphore_wait(barrier, expected)
    for k in sending:
        @pl.when(has[k])
        def _(k=k):
            v_copy(k, k ^ 1).start()

    loads[1].wait()
    for k in sending:
        @pl.when(has[k])
        def _(k=k):
            z_copy(k, k ^ 1).start()

        @pl.when(jnp.logical_not(has[k]))
        def _(k=k):
            far[k] = jnp.zeros(far.shape[1:], F32)
            basis[k] = jnp.zeros(basis.shape[1:], F32)

    own_basis = basis[own]
    basis_t = own_basis.T
    rows = basis_t.shape[0] // subs
    for half in range(2):
        ordered = jnp.concatenate(
            [basis_t[r * rows:(r + 1) * rows] for r in block_order(orders[half], subs)], axis=0
        )
        zt_hi[half], zt_lo[half] = split(ordered)

    all_modes = modes[...].reshape(-1, modes.shape[2])
    self_block = product(split(all_modes.T * stiffness[...]), split(all_modes))
    blocks[own] = self_block
    within = product(split(self_block), split(own_basis))

    def own_side(k, carry):
        pltpu.make_async_copy(couplings.at[k], tangent.at[k], tangent_sem.at[k]).wait()
        weight = present[0, k].astype(F32)
        value = product(split(tangent[k]), split(faces[k])) * weight
        turned_hi[k], turned_lo[k] = split(value.T)
        return carry

    lax.fori_loop(0, dirs, own_side, 0)

    for k in (0, 1, 2, 3, 4, 5):
        @pl.when(has[k])
        def _(k=k):
            v_copy(k, k).wait_recv()

        blocks[k] = product((turned_hi[k], turned_lo[k]), split(far[k]))
    blocks_copy = pltpu.make_async_copy(blocks, blocks_out, out_sem)
    blocks_copy.start()

    def projected(k):
        @pl.when(has[k])
        def _():
            z_copy(k, k).wait_recv()

        return product(split(blocks[k]), split(basis[k]))

    cols = basis.shape[2] // 2
    extent = acc[0].shape[1]

    def exchange(piece, half, t):
        bit = orders[half][t]
        mine = (sub // (1 << bit)) % 2
        length = extent // (2 << t)
        return pltpu.make_async_remote_copy(
            src_ref=acc[t].at[piece, pl.ds((1 - mine) * length, length)],
            dst_ref=got[t].at[piece], send_sem=r_send.at[t, piece], recv_sem=r_recv.at[t, piece],
            device_id=partners[bit], device_id_type=MESH,
        )

    pieces = []

    def begin(target, value):
        for half in range(2):
            piece = 2 * target + half
            part = split(value[:, half * cols:(half + 1) * cols])
            acc[0][piece] = product((zt_hi[half], zt_lo[half]), part)
            exchange(piece, half, 0).start()
            pieces.append((target, half, piece))

    begin(0, projected(4))
    begin(2, projected(5))
    for k in (0, 1, 2, 3):
        within = within + projected(k)
    begin(1, within)

    for t in range(bits):
        for target, half, piece in pieces:
            bit = orders[half][t]
            mine = (sub // (1 << bit)) % 2
            length = extent // (2 << t)
            exchange(piece, half, t).wait_recv()
            total = acc[t][piece, pl.ds(pl.multiple_of(mine * length, length), length)] + got[t][piece]
            if t < bits - 1:
                acc[t + 1][piece] = total
                exchange(piece, half, t + 1).start()
            else:
                group_out[target, :, half * cols:(half + 1) * cols] = total

    for k in sending:
        @pl.when(has[k])
        def _(k=k):
            v_copy(k, k ^ 1).wait_send()
            z_copy(k, k ^ 1).wait_send()
    for t in range(bits):
        for target, half, piece in pieces:
            exchange(piece, half, t).wait_send()
    blocks_copy.wait()


def body(groups, subs, couplings, mode_rows, coarse_basis, stiffness, own_face, neighbour_face, present):
    dirs, block = couplings.shape[1], couplings.shape[2]
    unknowns, modes = mode_rows.shape
    modes2 = coarse_basis.shape[1]
    bits = subs.bit_length() - 1
    rows = modes2 // subs
    cols = modes2 // 2
    any_space = pl.BlockSpec(memory_space=pl.ANY)
    smem = pl.BlockSpec(memory_space=pltpu.SMEM)
    vmem = pl.BlockSpec(memory_space=pltpu.VMEM)
    dma = pltpu.SemaphoreType.DMA
    work = 2 * dirs * block * modes * (block + modes) + 2 * unknowns * modes * modes
    blocks, rows_out = pl.pallas_call(
        functools.partial(kernel, groups, subs, dirs),
        out_shape=(
            jax.ShapeDtypeStruct((dirs + 1, modes, modes), F32),
            jax.ShapeDtypeStruct((3, rows, modes2), F32),
        ),
        in_specs=[smem, smem, any_space, any_space, any_space, vmem],
        out_specs=(any_space, vmem),
        scratch_shapes=[
            pltpu.VMEM((dirs, block, block), F32),
            pltpu.VMEM((unknowns // block, block, modes), F32),
            pltpu.VMEM((dirs, block, modes), F32),
            pltpu.VMEM((dirs, block, modes), F32),
            pltpu.VMEM((dirs + 1, modes, modes2), F32),
            pltpu.VMEM((dirs, modes, block), BF16),
            pltpu.VMEM((dirs, modes, block), BF16),
            pltpu.VMEM((2, modes2, modes), BF16),
            pltpu.VMEM((2, modes2, modes), BF16),
            pltpu.VMEM((dirs + 1, modes, modes), F32),
            [pltpu.VMEM((6, modes2 >> t, cols), F32) for t in range(bits)],
            [pltpu.VMEM((6, modes2 >> (t + 1), cols), F32) for t in range(bits)],
            dma((2,)), dma((dirs,)), dma,
            dma((dirs,)), dma((dirs,)), dma((dirs,)), dma((dirs,)),
            dma((bits, 6)), dma((bits, 6)),
        ],
        compiler_params=pltpu.CompilerParams(
            collective_id=0, has_side_effects=True, vmem_limit_bytes=56 * 1024 * 1024
        ),
        cost_estimate=pl.CostEstimate(
            flops=3 * work, bytes_accessed=4 * (dirs * block * block + unknowns * modes), transcendentals=0
        ),
    )(own_face, present, couplings[0], mode_rows.reshape(-1, block, modes), coarse_basis, stiffness)
    return (blocks[None], rows_out[None])


def solution(mesh):
    both = ("group", "sub")
    return jax.shard_map(
        functools.partial(body, mesh.shape["group"], mesh.shape["sub"]),
        mesh=mesh,
        in_specs=(P(both, None, None, None),) + (P(both, None),) * 6,
        out_specs=(P(both, None, None, None), P("group", None, "sub", None)),
        check_vma=False,
    )
```

time: 131 us -> 28.6 us (0.22)
  waiting for transfers between devices: 41.5 us -> 0 us
  starting transfers between devices: 34.5 us -> 0 us
  between operations: 25.8 us -> 0.64 us
  Pallas kernels: 0 us -> 24.4 us
  matrix products: 24.1 us -> 0 us
    reduce_scatter x1 -> x0, waiting for transfers between devices: 38.4 us -> none  [body(): own_rows = lax.psum_scatter(stacked, 'sub', scatter_dimension=1, tiled=True)]
    ppermute x12 -> x0, starting transfers between devices: 34.4 us -> none  [from_behind(): return lax.ppermute(shard, axis, pairs)]
    pallas_call x0 -> x1, Pallas kernels: none -> 24.4 us  [body(): pl.pallas_call(functools.partial(kernel, groups, subs, dirs), out_shape=(...]
    dot_general x27 -> x0, matrix products: 24.1 us -> none  [the longest x13 14.6 us: matmul(): jnp.dot(left, right, precision=PRECISE, preferred_element_type=jnp.float32)]
    slice x3 -> x0, local copies, waits for them, and re-layouts: 3.79 us -> none  [the longest x1 1.56 us: fetch_stack(): neighbour_face[0, direction] * block_size]
    unnamed x10 -> x2, local copies, waits for them, and re-layouts: 0.03 us -> 3.35 us
    ppermute x12 -> x0, waiting for transfers between devices: 3.12 us -> none  [from_behind(): return lax.ppermute(shard, axis, pairs)]
  transfers between devices with their start and end apart: 13 -> 0, of which waited for: 2 -> 0; matrix products, arithmetic and copies ran while one was open for 21% -> 0% of each run, Pallas kernels for 0% -> 0%
where the time goes in v1:
time: 28.6 us; the launch traced here: 28.4 us
  Pallas kernels  24.4 us (85%)
  local copies, waits for them, and re-layouts  3.35 us (12%)
  between operations  0.64 us (2%)
    pallas_call x1, Pallas kernels, body(): pl.pallas_call(functools.partial(kernel, groups, subs, dirs), out_shape=(...  24.4 us
    unnamed x2, local copies, waits for them, and re-layouts  3.35 us

profile of v1, /device:TPU:0, one launch (start us, length us, event | category | flops | bytes accessed | tf_op | source)
XLA Modules:
  0.0 28.4 jit_solution(12608648236475212856)
XLA Ops:
  0.6 24.4 %shard_map.77 = (f32[7,128,128]{2,1,0:T(8,128)}, f32[3,32,256]{2,1,0:T(8,128)}) custom-call(s32[1,6]{1,0:T(1,128)} %own_face.1, s32[1,6]{1,0:T(1,128)} %present.1, f32[6,384,384]{2,1,0:T(8,128)} %bitcast.4, f32[4,384,128]{2,1,0:T(8,128)} %bitcast.5, f32[128,256]{1,0:T(8,128)} %coarse_basis.1, f32[1,1536]{1,0:T(1,128)} %stiffness.1), custom_call_target="tpu_custom_call" | custom-call | flops 1056964608 | bytes 4325376 | tf_op jit(solution)/shard_map/pallas_call | solution.py:231
  25.0 1.8 %copy.10 = f32[1,7,128,128]{3,2,1,0:T(8,128)} copy(f32[1,7,128,128]{3,2,1,0:T(8,128)} %bitcast.6) | data formatting | bytes 917504
  26.8 1.5 %copy.11 = f32[1,3,32,256]{3,2,1,0:T(8,128)} copy(f32[1,3,32,256]{3,2,1,0:T(8,128)} %bitcast.7) | data formatting | bytes 196608

commit v2 on v1

--- a/solution.py
+++ b/solution.py
@@ -214,6 +214,17 @@
         for target, half, piece in pieces:
             exchange(piece, half, t).wait_send()
     blocks_copy.wait()
+
+
+def write_out(blocks, rows, blocks_out, rows_out, sem):
+    copies = [
+        pltpu.make_async_copy(blocks, blocks_out, sem.at[0]),
+        pltpu.make_async_copy(rows, rows_out, sem.at[1]),
+    ]
+    for copy in copies:
+        copy.start()
+    for copy in copies:
+        copy.wait()
 
 
 def body(groups, subs, couplings, mode_rows, coarse_basis, stiffness, own_face, neighbour_face, present):
@@ -260,6 +271,16 @@
             flops=3 * work, bytes_accessed=4 * (dirs * block * block + unknowns * modes), transcendentals=0
         ),
     )(own_face, present, couplings[0], mode_rows.reshape(-1, block, modes), coarse_basis, stiffness)
+    blocks, rows_out = pl.pallas_call(
+        write_out,
+        out_shape=(
+            jax.ShapeDtypeStruct(blocks.shape, F32),
+            jax.ShapeDtypeStruct(rows_out.shape, F32),
+        ),
+        in_specs=[vmem, vmem],
+        out_specs=(any_space, any_space),
+        scratch_shapes=[dma((2,))],
+    )(blocks, rows_out)
     return (blocks[None], rows_out[None])
 
 

time: 28.6 us -> 27.1 us (0.948)
  local copies, waits for them, and re-layouts: 3.35 us -> 0 us
  Pallas kernels: 24.4 us -> 26.2 us
    unnamed x2 -> x0, local copies, waits for them, and re-layouts: 3.35 us -> none
    pallas_call x0 -> x1, Pallas kernels: none -> 1.84 us  [body(): pl.pallas_call(write_out, out_shape=(jax.ShapeDtypeStruct(blocks.shape, F...]
where the time goes in v2:
time: 27.1 us; the launch traced here: 26.8 us
  Pallas kernels  26.2 us (97%)
  between operations  0.64 us (2%)
    pallas_call x1, Pallas kernels, body(): pl.pallas_call(functools.partial(kernel, groups, subs, dirs), out_shape=(...  24.4 us
    pallas_call x1, Pallas kernels, body(): pl.pallas_call(write_out, out_shape=(jax.ShapeDtypeStruct(blocks.shape, F...  1.84 us

profile of v2, /device:TPU:0, one launch (start us, length us, event | category | flops | bytes accessed | tf_op | source)
XLA Modules:
  0.0 26.8 jit_solution(13307332140320067981)
XLA Ops:
  0.6 24.4 %shard_map.77 = (f32[7,128,128]{2,1,0:T(8,128)}, f32[3,32,256]{2,1,0:T(8,128)}) custom-call(s32[1,6]{1,0:T(1,128)} %own_face.1, s32[1,6]{1,0:T(1,128)} %present.1, f32[6,384,384]{2,1,0:T(8,128)} %bitcast.4, f32[4,384,128]{2,1,0:T(8,128)} %bitcast.5, f32[128,256]{1,0:T(8,128)} %coarse_basis.1, f32[1,1536]{1,0:T(1,128)} %stiffness.1), custom_call_target="tpu_custom_call" | custom-call | flops 1056964608 | bytes 4325376 | tf_op jit(solution)/shard_map/pallas_call | solution.py:242
  25.0 1.8 %shard_map.78 = (f32[7,128,128]{2,1,0:T(8,128)}, f32[3,32,256]{2,1,0:T(8,128)}) custom-call(f32[7,128,128]{2,1,0:T(8,128)} %get-tuple-element.6.blocks, f32[3,32,256]{2,1,0:T(8,128)} %get-tuple-element.7.rows), custom_call_target="tpu_custom_call" | custom-call | tf_op jit(solution)/shard_map/pallas_call | solution.py:274
